TPU v7x, 32 devices: a whole 2x2x4 slice. The times are simulated.
32 devices in a mesh: grp: 2 (over y), tok: 4 (over z), sec: 2 (over core), ch: 2 (over x).
Axes of the slice: x: 2, y: 2, z: 4, core: 2. Of those that a mesh axis runs over, the one named last changes fastest.
Arguments:
- features: bfloat16 [4096, 2048], P('ch', ('grp', 'tok', 'sec')), parts along dimension 1, may hold values from -6 to 6
- gate_one: bfloat16 [4096, 2048], P('ch', ('grp', 'tok', 'sec')), parts along dimension 1, may hold values from -6 to 6
- taps_one: bfloat16 [4096, 128], P('ch'), may hold values from -0.5 to 0.5
- long_filter: bfloat16 [4096, 1024], P('ch', ('tok', 'sec')), may hold values from -0.1875 to 0.1875
- skip_gain: float32 [4096], P('ch'), may hold values from 0.5 to 1.5
- taps_two: bfloat16 [4096, 128], P('ch'), may hold values from -0.5 to 0.5
- gate_two: bfloat16 [4096, 2048], P('ch', ('grp', 'tok', 'sec')), parts along dimension 1, may hold values from -6 to 6
Outputs:
- mixed_out: bfloat16 [4096, 2048], P('ch', ('grp', 'tok', 'sec')), parts along dimension 1
There are 2 independent parts, one for each index of `grp`. A program takes and returns all parts, laid end to end along the dimension named above; an argument that names none is the same for every part. Nothing has to cross between parts.
All inputs are finite; a program needn't handle non-finite values.
Results may differ from a plain program's by a relative error of at most 0.0057.
Values may be sent and summed in bfloat16 or wider, within the bound.
A program may use at most 192 MiB of HBM per device.

v0:
```python
import math

import jax
import jax.numpy as jnp
from jax import lax
from jax.sharding import PartitionSpec as P


def passed_along(array, axis, by):
    length = lax.axis_size(axis)
    pairs = [(i, i + by) for i in range(length) if 0 <= i + by < length]
    return lax.ppermute(array, axis, pairs)


def depthwise(padded, kernel_taps):
    tap_count = kernel_taps.shape[1]
    length = padded.shape[1] - (tap_count - 1)
    group_size = 16
    total = jnp.zeros((padded.shape[0], length), jnp.float32)
    for first in range(0, tap_count, group_size):
        last = min(first + group_size, tap_count)
        stacked = jnp.stack(
            [padded[:, tap_count - 1 - k : tap_count - 1 - k + length] for k in range(first, last)],
            axis=1,
        )
        total = total + jnp.einsum(
            "cgl,cg->cl", stacked, kernel_taps[:, first:last], preferred_element_type=jnp.float32
        )
    return total


def angle_table(rows_count, cols_count, period):
    row_index = jnp.arange(rows_count, dtype=jnp.int32)[:, None]
    col_index = jnp.arange(cols_count, dtype=jnp.int32)[None, :]
    phase = (row_index * col_index % period).astype(jnp.float32) * (2.0 * math.pi / period)
    return (jnp.cos(phase), jnp.sin(phase))


def contract(form, left, right):
    return jnp.einsum(form, left, right, precision=lax.Precision.HIGHEST)


def forward_spectrum(signal, outer, inner, total):
    half_outer = outer // 2
    cos_first, sin_first = angle_table(half_outer, outer, outer)
    turn_cos, turn_sin = angle_table(outer, inner, total)
    cos_inner, sin_inner = angle_table(inner, inner, inner)
    shaped = signal.reshape(signal.shape[0], half_outer, inner)
    real_a = contract("cmn,mk->ckn", shaped, cos_first)
    imag_a = -contract("cmn,mk->ckn", shaped, sin_first)
    real_b = real_a * turn_cos + imag_a * turn_sin
    imag_b = imag_a * turn_cos - real_a * turn_sin
    real_c = contract("ckn,nj->cjk", real_b, cos_inner) + contract("ckn,nj->cjk", imag_b, sin_inner)
    imag_c = contract("ckn,nj->cjk", imag_b, cos_inner) - contract("ckn,nj->cjk", real_b, sin_inner)
    return (real_c, imag_c)


def inverse_spectrum(real_y, imag_y, outer, inner, total):
    half_outer = outer // 2
    cos_inner, sin_inner = angle_table(inner, inner, inner)
    turn_cos, turn_sin = angle_table(outer, inner, total)
    cos_last, sin_last = angle_table(outer, half_outer, outer)
    real_c = contract("cjk,jn->ckn", real_y, cos_inner) - contract("cjk,jn->ckn", imag_y, sin_inner)
    imag_c = contract("cjk,jn->ckn", imag_y, cos_inner) + contract("cjk,jn->ckn", real_y, sin_inner)
    real_d = real_c * turn_cos - imag_c * turn_sin
    imag_d = imag_c * turn_cos + real_c * turn_sin
    result = contract("ckn,km->cmn", real_d, cos_last) - contract("ckn,km->cmn", imag_d, sin_last)
    return (result / total).reshape(real_y.shape[0], half_outer * inner)


def on_device(features, gate_one, taps_one, long_filter, skip_gain, taps_two, gate_two):
    shards = lax.axis_size(("tok", "sec"))
    channels, block_len = features.shape
    narrow = channels // shards
    seq_len = block_len * shards
    rim_width = taps_one.shape[1] - 1
    total = 2 * seq_len
    inner = math.gcd(seq_len, 128)
    outer = total // inner
    filter_rows = lax.all_to_all(
        long_filter[:, None, :], ("tok", "sec"), split_axis=0, concat_axis=1, tiled=True
    ).reshape(narrow, seq_len)
    rim_rows = passed_along(features[:, block_len - rim_width :], ("tok", "sec"), 1)
    first_conv = depthwise(jnp.concatenate([rim_rows, features], axis=1), taps_one)
    mixed_one = (first_conv * gate_one).astype(jnp.bfloat16)
    channel_rows = lax.all_to_all(
        mixed_one[:, None, :], ("tok", "sec"), split_axis=0, concat_axis=1, tiled=True
    )
    channel_rows = channel_rows.reshape(narrow, seq_len).astype(jnp.float32)
    filter_real, filter_imag = forward_spectrum(
        filter_rows.astype(jnp.float32), outer, inner, total
    )
    signal_real, signal_imag = forward_spectrum(channel_rows, outer, inner, total)
    product_real = signal_real * filter_real - signal_imag * filter_imag
    product_imag = signal_real * filter_imag + signal_imag * filter_real
    conv_rows = inverse_spectrum(product_real, product_imag, outer, inner, total)
    skip_local = lax.dynamic_slice_in_dim(
        skip_gain, lax.axis_index(("tok", "sec")) * narrow, narrow
    )
    long_out = (conv_rows + skip_local[:, None] * channel_rows).astype(jnp.bfloat16)
    long_blocks = long_out.reshape(narrow, shards, block_len)
    tail_rows = jnp.concatenate(
        [
            jnp.zeros((narrow, 1, rim_width), jnp.bfloat16),
            long_blocks[:, :-1, block_len - rim_width :],
        ],
        axis=1,
    )
    windows = jnp.concatenate([tail_rows, long_blocks], axis=2)
    padded = lax.all_to_all(
        windows, ("tok", "sec"), split_axis=1, concat_axis=0, tiled=True
    ).reshape(channels, block_len + rim_width)
    second_conv = depthwise(padded, taps_two)
    return (second_conv * gate_two).astype(jnp.bfloat16)


def solution(mesh):
    in_specs = (
        P("ch", ("grp", "tok", "sec")),
        P("ch", ("grp", "tok", "sec")),
        P("ch", None),
        P("ch", ("tok", "sec")),
        P("ch"),
        P("ch", None),
        P("ch", ("grp", "tok", "sec")),
    )
    out_specs = P("ch", ("grp", "tok", "sec"))
    return jax.shard_map(
        on_device, mesh=mesh, in_specs=in_specs, out_specs=out_specs, check_vma=False
    )
```

profile of v0, /device:TPU:0, one launch (start us, length us, event | category | flops | bytes accessed | tf_op | source)
XLA Modules:
  0.0 428.3 jit_solution(18028862349489927458)
XLA Ops:
  8.1 6.1 %all-to-all-start.1 = ((bf16[8,2,16384]{2,1,0:T(2,128)(2,1)}), bf16[8,2,16384]{2,1,0:T(2,128)(2,1)S(1)}, u32[]{:S(2)}, u32[]{:S(2)}) async-start(bf16[8,2,16384]{2,1,0:T(2,128)(2,1)} %reshape.112), calls=%async_computation.1 | async-start | bytes 1048576 | tf_op jit(solution)/shard_map/all_to_all | solution.py:80
  14.3 5.7 %slice_bitcast_fusion.142 = (bf16[2048,16,1]{1,0,2:T(8,128)(2,1)S(1)}, bf16[2048,16,1]{1,0,2:T(8,128)(2,1)}, bf16[2048,16,1]{1,0,2:T(8,128)(2,1)}, bf16[2048,16,...) fusion(bf16[2048,128]{1,0:T(8,128)(2,1)} %param.9), kind=kLoop, calls=%fused_computation.1013 | loop fusion | bytes 1048576 | tf_op jit(solution)/shard_map/slice | solution.py:27
  28.0 3.2 copy-done.13
  31.2 3.5 constant_dynamic-update-slice_fusion.16
  50.5 3.0 constant_dynamic-update-slice_fusion
  59.8 3.5 constant_dynamic-update-slice_fusion.32
  110.5 8.7 %fusion.16 = f32[2048,1,128]{2,1,0:T(1,128)S(1)} fusion(bf16[2048,16,128]{2,0,1:T(8,128)(2,1)} %constant_dynamic-update-slice_fusion.112, bf16[2048,16,1]{1,0,2:T(8,128)(2,1)S(1)} %get-tuple-element.191), kind=kOutput, calls=%fused_computation.268 | convolution fusion | flops 8388608 | bytes 9502720 | tf_op jit(solution)/shard_map/cgl,cg->cl/dot_general | solution.py:26
  119.2 8.7 %fusion.18 = f32[2048,1,128]{2,1,0:T(1,128)S(1)} fusion(bf16[2048,16,128]{2,0,1:T(8,128)(2,1)} %get-tuple-element.175, bf16[2048,16,1]{1,0,2:T(8,128)(2,1)S(1)} %get-tuple-element.192), kind=kOutput, calls=%fused_computation.270 | convolution fusion | flops 8388608 | bytes 9502720 | tf_op jit(solution)/shard_map/cgl,cg->cl/dot_general | solution.py:26
  127.9 9.2 %fusion.20 = f32[2048,1,128]{2,1,0:T(1,128)S(1)} fusion(bf16[2048,16,128]{2,0,1:T(8,128)(2,1)} %copy-done.9, bf16[2048,16,1]{1,0,2:T(8,128)(2,1)} %get-tuple-element.186), kind=kOutput, calls=%fused_computation.272 | convolution fusion | flops 8388608 | bytes 9502720 | tf_op jit(solution)/shard_map/cgl,cg->cl/dot_general | solution.py:26
  137.1 9.8 %fusion.22 = f32[2048,1,128]{2,1,0:T(1,128)} fusion(bf16[2048,16,128]{2,0,1:T(8,128)(2,1)} %copy-done.8, bf16[2048,16,1]{1,0,2:T(8,128)(2,1)} %get-tuple-element.187), kind=kOutput, calls=%fused_computation.274 | convolution fusion | flops 8388608 | bytes 9502720 | tf_op jit(solution)/shard_map/cgl,cg->cl/dot_general | solution.py:26
  146.9 10.0 %fusion.24 = f32[2048,1,128]{2,1,0:T(1,128)} fusion(bf16[2048,16,128]{2,0,1:T(8,128)(2,1)} %copy-done.7, bf16[2048,16,1]{1,0,2:T(8,128)(2,1)} %get-tuple-element.188), kind=kOutput, calls=%fused_computation.276 | convolution fusion | flops 8388608 | bytes 9502720 | tf_op jit(solution)/shard_map/cgl,cg->cl/dot_general | solution.py:26
  156.8 9.8 %fusion.26 = f32[2048,1,128]{2,1,0:T(1,128)} fusion(bf16[2048,16,128]{2,0,1:T(8,128)(2,1)} %copy-done.6, bf16[2048,16,1]{1,0,2:T(8,128)(2,1)} %get-tuple-element.189), kind=kOutput, calls=%fused_computation.278 | convolution fusion | flops 8388608 | bytes 9502720 | tf_op jit(solution)/shard_map/cgl,cg->cl/dot_general | solution.py:26
  166.6 10.1 %fusion.30 = f32[2048,1,128]{2,1,0:T(1,128)} fusion(bf16[2048,16,128]{2,0,1:T(8,128)(2,1)} %get-tuple-element.149, bf16[2048,16,1]{1,0,2:T(8,128)(2,1)S(1)} %get-tuple-element.190), kind=kOutput, calls=%fused_computation.282 | convolution fusion | flops 8388608 | bytes 9502720 | tf_op jit(solution)/shard_map/cgl,cg->cl/dot_general | solution.py:26
  176.7 9.8 %fusion.28 = f32[2048,1,128]{2,1,0:T(1,128)} fusion(bf16[2048,16,128]{2,0,1:T(8,128)(2,1)} %get-tuple-element.141, bf16[2048,16,1]{1,0,2:T(8,128)(2,1)S(1)} %get-tuple-element.185), kind=kOutput, calls=%fused_computation.280 | convolution fusion | flops 8388608 | bytes 9502720 | tf_op jit(solution)/shard_map/cgl,cg->cl/dot_general | solution.py:26
  191.4 5.1 %all-to-all-start = ((bf16[8,2,16384]{2,1,0:T(2,128)(2,1)}), bf16[8,2,16384]{2,1,0:T(2,128)(2,1)}, u32[]{:S(2)}, u32[]{:S(2)}) async-start(bf16[8,2,16384]{2,1,0:T(2,128)(2,1)} %reshape.110), calls=%async_computation | async-start | bytes 1048576 | tf_op jit(solution)/shard_map/all_to_all | solution.py:86
  201.5 10.5 %all-to-all-done = bf16[8,2,16384]{2,1,0:T(2,128)(2,1)} async-done(((bf16[8,2,16384]{2,1,0:T(2,128)(2,1)}), bf16[8,2,16384]{2,1,0:T(2,128)(2,1)}, u32[]{:S(2)}, u32[]{:S(2)}) %all-to-all-start) | async-done | bytes 524320 | tf_op jit(solution)/shard_map/all_to_all | solution.py:86
  215.6 3.5 add_bitcast_fusion
  237.9 3.5 multiply_subtract_fusion.1
  241.4 3.6 fusion.34
  245.0 3.6 fusion.32
  248.6 3.7 fusion.73
  252.3 3.8 multiply_subtract_fusion
  263.0 3.8 all-to-all-start.2
  269.5 23.6 %all-to-all-done.2 = bf16[256,8,255]{2,0,1:T(8,128)(2,1)S(1)} async-done(((bf16[256,8,255]{2,0,1:T(8,128)(2,1)}), bf16[256,8,255]{2,0,1:T(8,128)(2,1)S(1)}, u32[]{:S(2)}, u32[]{:S(2)}) %all-to-all-start.2) | async-done | bytes 1044512 | tf_op jit(solution)/shard_map/all_to_all | solution.py:110
  295.9 3.0 constant_dynamic-update-slice_fusion.158
  298.9 3.0 constant_dynamic-update-slice_fusion.157
  301.9 3.0 constant_dynamic-update-slice_fusion.156
  304.9 3.0 constant_dynamic-update-slice_fusion.155
  307.9 3.1 constant_dynamic-update-slice_fusion.154
  311.0 3.0 constant_dynamic-update-slice_fusion.153
  314.0 3.0 constant_dynamic-update-slice_fusion.152
  317.0 3.1 constant_dynamic-update-slice_fusion.151
  320.1 3.4 constant_dynamic-update-slice_fusion.150
  323.5 3.0 constant_dynamic-update-slice_fusion.149
  326.4 3.1 constant_dynamic-update-slice_fusion.148
  329.5 3.0 constant_dynamic-update-slice_fusion.147
  332.5 3.0 constant_dynamic-update-slice_fusion.146
  335.5 3.0 constant_dynamic-update-slice_fusion.145
  341.4 3.2 copy-done.10
  349.6 8.9 %fusion.14 = f32[2048,1,128]{2,1,0:T(1,128)S(1)} fusion(bf16[2048,16,128]{2,0,1:T(8,128)(2,1)} %get-tuple-element.20, bf16[2048,16,1]{1,0,2:T(8,128)(2,1)S(1)} %copy-done.5), kind=kOutput, calls=%fused_computation.266 | convolution fusion | flops 8388608 | bytes 9502720 | tf_op jit(solution)/shard_map/cgl,cg->cl/dot_general | solution.py:26
  358.5 8.7 %fusion.12 = f32[2048,1,128]{2,1,0:T(1,128)S(1)} fusion(bf16[2048,16,128]{2,0,1:T(8,128)(2,1)} %copy-done.10, bf16[2048,16,1]{1,0,2:T(8,128)(2,1)S(1)} %copy-done.4), kind=kOutput, calls=%fused_computation.264 | convolution fusion | flops 8388608 | bytes 9502720 | tf_op jit(solution)/shard_map/cgl,cg->cl/dot_general | solution.py:26
  367.2 8.9 %fusion.10 = f32[2048,1,128]{2,1,0:T(1,128)S(1)} fusion(bf16[2048,16,128]{2,0,1:T(8,128)(2,1)} %get-tuple-element.19, bf16[2048,16,1]{1,0,2:T(8,128)(2,1)S(1)} %get-tuple-element.181), kind=kOutput, calls=%fused_computation.262 | convolution fusion | flops 8388608 | bytes 9502720 | tf_op jit(solution)/shard_map/cgl,cg->cl/dot_general | solution.py:26
  376.2 8.8 %fusion.8 = f32[2048,1,128]{2,1,0:T(1,128)S(1)} fusion(bf16[2048,16,128]{2,0,1:T(8,128)(2,1)} %get-tuple-element.18, bf16[2048,16,1]{1,0,2:T(8,128)(2,1)} %get-tuple-element.180), kind=kOutput, calls=%fused_computation.260 | convolution fusion | flops 8388608 | bytes 9502720 | tf_op jit(solution)/shard_map/cgl,cg->cl/dot_general | solution.py:26
  385.0 10.1 %fusion.6 = f32[2048,1,128]{2,1,0:T(1,128)} fusion(bf16[2048,16,128]{2,0,1:T(8,128)(2,1)} %get-tuple-element.17, bf16[2048,16,1]{1,0,2:T(8,128)(2,1)} %get-tuple-element.179), kind=kOutput, calls=%fused_computation.258 | convolution fusion | flops 8388608 | bytes 9502720 | tf_op jit(solution)/shard_map/cgl,cg->cl/dot_general | solution.py:26
  395.1 9.8 %fusion.4 = f32[2048,1,128]{2,1,0:T(1,128)} fusion(bf16[2048,16,128]{2,0,1:T(8,128)(2,1)} %get-tuple-element.16, bf16[2048,16,1]{1,0,2:T(8,128)(2,1)} %get-tuple-element.178), kind=kOutput, calls=%fused_computation.256 | convolution fusion | flops 8388608 | bytes 9502720 | tf_op jit(solution)/shard_map/cgl,cg->cl/dot_general | solution.py:26
  404.8 9.7 %fusion.2 = f32[2048,1,128]{2,1,0:T(1,128)} fusion(bf16[2048,16,128]{2,0,1:T(8,128)(2,1)} %copy-done.12, bf16[2048,16,1]{1,0,2:T(8,128)(2,1)S(1)} %get-tuple-element.184), kind=kOutput, calls=%fused_computation.254 | convolution fusion | flops 8388608 | bytes 9502720 | tf_op jit(solution)/shard_map/cgl,cg->cl/dot_general | solution.py:26
  414.5 10.0 %fusion = f32[2048,1,128]{2,1,0:T(1,128)} fusion(bf16[2048,16,128]{2,0,1:T(8,128)(2,1)} %copy-done.11, bf16[2048,16,1]{1,0,2:T(8,128)(2,1)} %get-tuple-element.183), kind=kOutput, calls=%fused_computation.252 | convolution fusion | flops 8388608 | bytes 9502720 | tf_op jit(solution)/shard_map/cgl,cg->cl/dot_general | solution.py:26
  424.5 3.6 multiply_convert_fusion
  (156 shorter events, 137.6 us)
Async XLA Ops:
  0.0 20.0 %copy-start = (bf16[2048,128]{1,0:T(8,128)(2,1)S(1)}, bf16[2048,128]{1,0:T(8,128)(2,1)}, u32[]{:S(2)}) copy-start(bf16[2048,128]{1,0:T(8,128)(2,1)} %param.7) | copy-start | bytes 1572868
  2.1 17.8 %collective-permute-start = (bf16[2048,127]{1,0:T(8,128)(2,1)}, bf16[2048,127]{1,0:T(8,128)(2,1)S(1)}, u32[]{:S(2)}, u32[]{:S(2)}) collective-permute-start(bf16[2048,127]{1,0:T(8,128)(2,1)} %slice.819), channel_id=1, source_target_pairs={{0,2},{2,4},{4,6},{6,8},{8,10},{10,12},{12,14},{1,3},{3,5},{5,7},{... | collective-permute-start | bytes 1560584 | tf_op jit(solution)/shard_map/ppermute | solution.py:12
  8.1 183.3 %all-to-all-start.1 = ((bf16[8,2,16384]{2,1,0:T(2,128)(2,1)}), bf16[8,2,16384]{2,1,0:T(2,128)(2,1)S(1)}, u32[]{:S(2)}, u32[]{:S(2)}) async-start(bf16[8,2,16384]{2,1,0:T(2,128)(2,1)} %reshape.112), calls=%async_computation.1 | async-start | bytes 1048576 | tf_op jit(solution)/shard_map/all_to_all | solution.py:80
  28.0 3.2 copy-start.13
  63.3 5.3 %copy-start.6 = (bf16[2048,16,128]{2,0,1:T(8,128)(2,1)}, bf16[2048,16,128]{2,0,1:T(8,128)(2,1)S(1)}, u32[]{:S(2)}) copy-start(bf16[2048,16,128]{2,0,1:T(8,128)(2,1)S(1)} %get-tuple-element.157) | copy-start | bytes 25165828
  71.9 5.3 %copy-start.7 = (bf16[2048,16,128]{2,0,1:T(8,128)(2,1)}, bf16[2048,16,128]{2,0,1:T(8,128)(2,1)S(1)}, u32[]{:S(2)}) copy-start(bf16[2048,16,128]{2,0,1:T(8,128)(2,1)S(1)} %get-tuple-element.163) | copy-start | bytes 25165828
  79.6 7.1 %copy-start.8 = (bf16[2048,16,128]{2,0,1:T(8,128)(2,1)}, bf16[2048,16,128]{2,0,1:T(8,128)(2,1)S(1)}, u32[]{:S(2)}) copy-start(bf16[2048,16,128]{2,0,1:T(8,128)(2,1)S(1)} %get-tuple-element.168) | copy-start | bytes 25165828
  86.6 14.3 %copy-start.9 = (bf16[2048,16,128]{2,0,1:T(8,128)(2,1)}, bf16[2048,16,128]{2,0,1:T(8,128)(2,1)S(1)}, u32[]{:S(2)}) copy-start(bf16[2048,16,128]{2,0,1:T(8,128)(2,1)S(1)} %get-tuple-element.172) | copy-start | bytes 25165828
  176.7 9.8 %copy-start.2 = (bf16[2048,128]{1,0:T(8,128)(2,1)S(1)}, bf16[2048,128]{1,0:T(8,128)(2,1)}, u32[]{:S(2)}) copy-start(bf16[2048,128]{1,0:T(8,128)(2,1)} %param.8) | copy-start | bytes 1572868
  191.4 20.6 %all-to-all-start = ((bf16[8,2,16384]{2,1,0:T(2,128)(2,1)}), bf16[8,2,16384]{2,1,0:T(2,128)(2,1)}, u32[]{:S(2)}, u32[]{:S(2)}) async-start(bf16[8,2,16384]{2,1,0:T(2,128)(2,1)} %reshape.110), calls=%async_computation | async-start | bytes 1048576 | tf_op jit(solution)/shard_map/all_to_all | solution.py:86
  256.1 10.7 %copy-start.1 = (bf16[2048,128]{1,0:T(8,128)(2,1)S(1)}, bf16[2048,128]{1,0:T(8,128)(2,1)}, u32[]{:S(2)}) copy-start(bf16[2048,128]{1,0:T(8,128)(2,1)} %param.12) | copy-start | bytes 1572868
  263.0 30.1 %all-to-all-start.2 = ((bf16[256,8,255]{2,0,1:T(8,128)(2,1)}), bf16[256,8,255]{2,0,1:T(8,128)(2,1)S(1)}, u32[]{:S(2)}, u32[]{:S(2)}) async-start(bf16[256,8,255]{2,0,1:T(8,128)(2,1)} %copy.106), calls=%async_computation.2 | async-start | bytes 2097152 | tf_op jit(solution)/shard_map/all_to_all | solution.py:110
  335.5 14.1 %copy-start.5 = (bf16[2048,16,1]{1,0,2:T(8,128)(2,1)S(1)}, bf16[2048,16,1]{1,0,2:T(8,128)(2,1)}, u32[]{:S(2)}) copy-start(bf16[2048,16,1]{1,0,2:T(8,128)(2,1)} %get-tuple-element.182) | copy-start | bytes 196612
  341.4 3.2 copy-start.10
  341.4 5.8 %copy-start.11 = (bf16[2048,16,128]{2,0,1:T(8,128)(2,1)}, bf16[2048,16,128]{2,0,1:T(8,128)(2,1)S(1)}, u32[]{:S(2)}) copy-start(bf16[2048,16,128]{2,0,1:T(8,128)(2,1)S(1)} %get-tuple-element.14) | copy-start | bytes 25165828
  341.4 8.2 %copy-start.12 = (bf16[2048,16,128]{2,0,1:T(8,128)(2,1)}, bf16[2048,16,128]{2,0,1:T(8,128)(2,1)S(1)}, u32[]{:S(2)}) copy-start(bf16[2048,16,128]{2,0,1:T(8,128)(2,1)S(1)} %get-tuple-element.15) | copy-start | bytes 25165828
  341.4 17.1 %copy-start.4 = (bf16[2048,16,1]{1,0,2:T(8,128)(2,1)S(1)}, bf16[2048,16,1]{1,0,2:T(8,128)(2,1)}, u32[]{:S(2)}) copy-start(bf16[2048,16,1]{1,0,2:T(8,128)(2,1)} %get-tuple-element.177) | copy-start | bytes 196612
  414.5 10.0 %copy-start.3 = (bf16[2048,128]{1,0:T(8,128)(2,1)S(1)}, bf16[2048,128]{1,0:T(8,128)(2,1)}, u32[]{:S(2)}) copy-start(bf16[2048,128]{1,0:T(8,128)(2,1)} %param.13) | copy-start | bytes 1572868
where the time goes:
time: 436 us; the launch traced here: 428 us
  matrix products  201 us (46%)
  other arithmetic  97.4 us (22%)
  local copies, waits for them, and re-layouts  78 us (18%)
  waiting for transfers between devices  34.1 us (8%)
  starting transfers between devices  17.4 us (4%)
    dot_general x16, matrix products, depthwise(): jnp.einsum('cgl,cg->cl', stacked, kernel_taps[:, first:last], preferred_e...  151 us
    unnamed x91, other arithmetic  67.3 us
    unnamed x49, local copies, waits for them, and re-layouts  61.9 us
    dot_general x18, matrix products, contract(): return jnp.einsum(form, left, right, precision=lax.Precision.HIGHEST)  50 us
    all_to_all x1, waiting for transfers between devices, on_device(): lax.all_to_all(windows, ('tok', 'sec'), split_axis=1, concat_axis=0, tile...  23.6 us
    another operation x8, other arithmetic, depthwise(): jnp.stack([padded[:, tap_count - 1 - k:tap_count - 1 - k + length] for k...  19.8 us
    all_to_all x1, waiting for transfers between devices, on_device(): lax.all_to_all(mixed_one[:, None, :], ('tok', 'sec'), split_axis=0, conca...  10.5 us
  transfers between devices with their start and end apart: 4, of which 2 were waited for; matrix products, arithmetic and copies ran while one was open for 43% of the time, Pallas kernels for 0%

commit v1 on v0

v1 whole, which is shorter than its diff:
```python
import math

import jax
import jax.numpy as jnp
import ml_dtypes
import numpy as np
from jax import lax
from jax.sharding import PartitionSpec as P

RING = ("tok", "sec")
TABLE_LIMIT = 1 << 23


def angles(tokens, half):
    steps = (np.arange(tokens)[:, None] * (2 * np.arange(half)[None, :] + 1)) % (4 * half)
    return steps * (math.pi / (2 * half))


def two_pieces(table):
    high = table.astype(ml_dtypes.bfloat16)
    low = (table - high.astype(np.float64)).astype(ml_dtypes.bfloat16)
    return high, low


def forward_table(tokens, half):
    angle = angles(tokens, half)
    return two_pieces(np.concatenate([np.cos(angle), -np.sin(angle)], axis=1))


def backward_table(tokens, half):
    angle = angles(tokens, half).T
    return two_pieces(np.concatenate([np.cos(angle), -np.sin(angle)], axis=0) / half)


def dot(left, right):
    return jnp.dot(left, right, preferred_element_type=jnp.float32)


def forward(signal, table):
    return dot(signal, table[0]) + dot(signal, table[1])


def backward(spectrum, table):
    high = spectrum.astype(jnp.bfloat16)
    low = (spectrum - high.astype(jnp.float32)).astype(jnp.bfloat16)
    return dot(high, table[0]) + dot(low, table[0]) + dot(high, table[1])


def times(left, right):
    half = left.shape[1] // 2
    a, b = left[:, :half], left[:, half:]
    c, d = right[:, :half], right[:, half:]
    return jnp.concatenate([a * c - b * d, a * d + b * c], axis=1)


def short_conv(before, block, taps):
    length = taps.shape[1]
    table = forward_table(2 * length, length)
    back = backward_table(2 * length, length)
    early = tuple(piece[:length] for piece in table)
    late = tuple(piece[length:] for piece in table)
    spectrum = forward(before, early) + forward(block, late)
    product = times(spectrum, forward(taps, early))
    return backward(product, tuple(piece[:, length:] for piece in back))


def angle_table(rows_count, cols_count, period):
    row_index = jnp.arange(rows_count, dtype=jnp.int32)[:, None]
    col_index = jnp.arange(cols_count, dtype=jnp.int32)[None, :]
    phase = (row_index * col_index % period).astype(jnp.float32) * (2.0 * math.pi / period)
    return (jnp.cos(phase), jnp.sin(phase))


def contract(form, left, right):
    return jnp.einsum(form, left, right, precision=lax.Precision.HIGHEST)


def forward_spectrum(signal, outer, inner, total):
    half_outer = outer // 2
    cos_first, sin_first = angle_table(half_outer, outer, outer)
    turn_cos, turn_sin = angle_table(outer, inner, total)
    cos_inner, sin_inner = angle_table(inner, inner, inner)
    shaped = signal.reshape(signal.shape[0], half_outer, inner)
    real_a = contract("cmn,mk->ckn", shaped, cos_first)
    imag_a = -contract("cmn,mk->ckn", shaped, sin_first)
    real_b = real_a * turn_cos + imag_a * turn_sin
    imag_b = imag_a * turn_cos - real_a * turn_sin
    real_c = contract("ckn,nj->cjk", real_b, cos_inner) + contract("ckn,nj->cjk", imag_b, sin_inner)
    imag_c = contract("ckn,nj->cjk", imag_b, cos_inner) - contract("ckn,nj->cjk", real_b, sin_inner)
    return (real_c, imag_c)


def inverse_spectrum(real_y, imag_y, outer, inner, total):
    half_outer = outer // 2
    cos_inner, sin_inner = angle_table(inner, inner, inner)
    turn_cos, turn_sin = angle_table(outer, inner, total)
    cos_last, sin_last = angle_table(outer, half_outer, outer)
    real_c = contract("cjk,jn->ckn", real_y, cos_inner) - contract("cjk,jn->ckn", imag_y, sin_inner)
    imag_c = contract("cjk,jn->ckn", imag_y, cos_inner) + contract("cjk,jn->ckn", real_y, sin_inner)
    real_d = real_c * turn_cos - imag_c * turn_sin
    imag_d = imag_c * turn_cos + real_c * turn_sin
    result = contract("ckn,km->cmn", real_d, cos_last) - contract("ckn,km->cmn", imag_d, sin_last)
    return (result / total).reshape(real_y.shape[0], half_outer * inner)


def factored_pair(signal, filter_rows, skip, taps):
    channels, seq_len = signal.shape
    length = taps.shape[1]
    total = 2 * seq_len
    inner = math.gcd(seq_len, 128)
    outer = total // inner
    wide = signal.astype(jnp.float32)
    a, b = forward_spectrum(wide, outer, inner, total)
    c, d = forward_spectrum(filter_rows.astype(jnp.float32), outer, inner, total)
    rows = inverse_spectrum(a * c - b * d, a * d + b * c, outer, inner, total) + skip * wide
    rows = rows.astype(jnp.bfloat16)
    blocks = seq_len // length
    before = jnp.pad(rows, ((0, 0), (length, 0)))[:, :seq_len]
    result = short_conv(
        before.reshape(channels * blocks, length),
        rows.reshape(channels * blocks, length),
        jnp.repeat(taps, blocks, axis=0),
    )
    return result.reshape(channels, seq_len)


def dense_pair(signal, filter_rows, skip, taps, half):
    seq_len = signal.shape[1]
    table = forward_table(seq_len, half)
    weights = forward(filter_rows, table)
    weights = jnp.concatenate([weights[:, :half] + skip, weights[:, half:]], axis=1)
    weights = times(weights, forward(taps, tuple(piece[: taps.shape[1]] for piece in table)))
    return backward(times(forward(signal, table), weights), backward_table(seq_len, half))


def exchange(blocks):
    return lax.all_to_all(blocks, RING, split_axis=0, concat_axis=0, tiled=True)


def on_device(features, gate_one, taps_one, long_filter, skip_gain, taps_two, gate_two):
    shards = lax.axis_size(RING)
    channels, block_len = features.shape
    narrow = channels // shards
    seq_len = block_len * shards
    length = taps_one.shape[1]

    def rows_of(blocks):
        return jnp.swapaxes(blocks, 0, 1).reshape(narrow, seq_len)

    filter_rows = rows_of(exchange(long_filter.reshape(shards, narrow, block_len)))
    before = lax.ppermute(features, RING, [(i, i + 1) for i in range(shards - 1)])
    mixed_one = (short_conv(before, features, taps_one) * gate_one).astype(jnp.bfloat16)
    signal = rows_of(exchange(mixed_one.reshape(shards, narrow, block_len)))
    first = lax.axis_index(RING) * narrow
    skip = lax.dynamic_slice_in_dim(skip_gain, first, narrow)[:, None]
    taps = lax.dynamic_slice_in_dim(taps_two, first, narrow)
    half = -(-(2 * seq_len + length) // 256) * 128
    if seq_len * half <= TABLE_LIMIT:
        result = dense_pair(signal, filter_rows, skip, taps, half)
    else:
        result = factored_pair(signal, filter_rows, skip, taps)
    result = result.astype(jnp.bfloat16).reshape(narrow, shards, block_len)
    second_conv = exchange(jnp.swapaxes(result, 0, 1)).reshape(channels, block_len)
    return (second_conv.astype(jnp.float32) * gate_two).astype(jnp.bfloat16)


def solution(mesh):
    in_specs = (
        P("ch", ("grp", "tok", "sec")),
        P("ch", ("grp", "tok", "sec")),
        P("ch", None),
        P("ch", ("tok", "sec")),
        P("ch"),
        P("ch", None),
        P("ch", ("grp", "tok", "sec")),
    )
    out_specs = P("ch", ("grp", "tok", "sec"))
    return jax.shard_map(
        on_device, mesh=mesh, in_specs=in_specs, out_specs=out_specs, check_vma=False
    )
```

time: 436 us -> 83.4 us (0.19); the launches traced: 428 us -> 82.6 us
  matrix products: 201 us -> 26.3 us
  other arithmetic: 97.4 us -> 2.16 us
  local copies, waits for them, and re-layouts: 78 us -> 7.86 us
  waiting for transfers between devices: 34.1 us -> 7.07 us
  blocking collectives: 0 us -> 17.9 us
    dot_general x34 -> x18, matrix products: 201 us -> 26.3 us  [dot(): return jnp.dot(left, right, preferred_element_type=jnp.float32)]
    unnamed x91 -> x4, other arithmetic: 67.3 us -> 0.01 us
    unnamed x49 -> x44, local copies, waits for them, and re-layouts: 61.9 us -> 4.69 us
    all_to_all x3 -> x2, waiting for transfers between devices: 34.1 us -> 7.07 us  [exchange(): return lax.all_to_all(blocks, RING, split_axis=0, concat_axis=0, tiled=True)]
    another operation x8 -> x0, other arithmetic: 19.8 us -> none  [depthwise(): jnp.stack([padded[:, tap_count - 1 - k:tap_count - 1 - k + length] for k...]
    all_to_all x0 -> x1, blocking collectives: none -> 17.9 us  [exchange(): return lax.all_to_all(blocks, RING, split_axis=0, concat_axis=0, tiled=True)]
    slice x4 -> x0, local copies, waits for them, and re-layouts: 10.7 us -> none  [the longest x2 8.38 us: depthwise(): kernel_taps[:, first:last]]
    broadcast_in_dim x3 -> x0, other arithmetic: 6.11 us -> none  [the longest x2 4.01 us: on_device(): mixed_one[:, None, :]]
  transfers between devices with their start and end apart: 4 -> 3, of which waited for: 2 -> 1; matrix products, arithmetic and copies ran while one was open for 43% -> 24% of each run, Pallas kernels for 0% -> 0%
where the time goes in v1:
time: 83.4 us; the launch traced here: 82.6 us
  matrix products  26.3 us (32%)
  starting transfers between devices  21 us (25%)
  blocking collectives  17.9 us (21%)
  local copies, waits for them, and re-layouts  7.86 us (9%)
  waiting for transfers between devices  7.07 us (8%)
  other arithmetic  2.16 us (3%)
    dot_general x18, matrix products, dot(): return jnp.dot(left, right, preferred_element_type=jnp.float32)  26.3 us
    all_to_all x1, blocking collectives, exchange(): return lax.all_to_all(blocks, RING, split_axis=0, concat_axis=0, tiled=True)  17.9 us
    all_to_all x2, starting transfers between devices, exchange(): return lax.all_to_all(blocks, RING, split_axis=0, concat_axis=0, tiled=True)  17.8 us
    all_to_all x2, waiting for transfers between devices, exchange(): return lax.all_to_all(blocks, RING, split_axis=0, concat_axis=0, tiled=True)  7.07 us
    unnamed x44, local copies, waits for them, and re-layouts  4.69 us
    ppermute x1, starting transfers between devices, on_device(): lax.ppermute(features, RING, [(i, i + 1) for i in range(shards - 1)])  3.2 us
  transfers between devices with their start and end apart: 3, of which 1 were waited for; matrix products, arithmetic and copies ran while one was open for 24% of the time, Pallas kernels for 0%

profile of v1, /device:TPU:0, one launch (start us, length us, event | category | flops | bytes accessed | tf_op | source)
XLA Modules:
  0.0 82.6 jit_solution(8324076991710264321)
XLA Ops:
  0.0 6.5 %all-to-all-start.1 = ((bf16[8,256,128]{2,1,0:T(8,128)(2,1)}), bf16[8,256,128]{2,1,0:T(8,128)(2,1)}, u32[]{:S(2)}, u32[]{:S(2)}) async-start(bf16[8,256,128]{2,1,0:T(8,128)(2,1)} %bitcast.62), calls=%async_computation.1 | async-start | bytes 1048576 | tf_op jit(solution)/shard_map/all_to_all | solution.py:137
  6.5 3.2 %collective-permute-start = (bf16[2048,128]{1,0:T(8,128)(2,1)}, bf16[2048,128]{1,0:T(8,128)(2,1)}, u32[]{:S(2)}, u32[]{:S(2)}) collective-permute-start(bf16[2048,128]{1,0:T(8,128)(2,1)} %param.19), channel_id=1, source_target_pairs={{0,2},{2,4},{4,6},{6,8},{8,10},{10,12},{12,14},{1,3},{3,5},{5,7},{... | collective-permute-start | bytes 1572872 | tf_op jit(solution)/shard_map/ppermute | solution.py:151
  9.7 1.5 %fusion.31 = f32[256,2048]{1,0:T(8,128)S(1)} fusion(bf16[128,256]{1,0:T(8,128)(2,1)} %constant.43.clone, bf16[2048,128]{1,0:T(8,128)(2,1)} %param.19), kind=kOutput, calls=%fused_computation.48 | convolution fusion | flops 134217728 | bytes 2686976 | tf_op jit(solution)/shard_map/dot_general | solution.py:36
  11.2 0.8 dynamic_slice.6
  12.0 0.5 convolution_add_fusion.4
  12.5 0.6 copy-done.3
  13.0 0.5 fusion.32
  13.5 0.4 copy-done.11
  13.9 0.5 fusion.1
  14.3 0.6 copy-done.5
  14.9 0.5 fusion.20
  15.4 0.6 copy-done.6
  16.0 1.9 %convolution_add_fusion = f32[256,2304]{1,0:T(8,128)} fusion(f32[256,2304]{1,0:T(8,128)S(1)} %fusion.20, bf16[128,2304]{1,0:T(8,128)(2,1)S(1)} %copy-done.6, bf16[2048,128]{1,0:T(8,128)(2,1)S(1)} %copy-done, s32[]{:T(128)S(6)} %select_n.4), kind=kOutput, calls=%fused_computation | convolution fusion | flops 151584768 | bytes 5373956 | tf_op jit(solution)/shard_map/dot_general | solution.py:36
  17.9 1.5 %fusion.30 = f32[256,2048]{1,0:T(8,128)S(1)} fusion(bf16[128,256]{1,0:T(8,128)(2,1)S(1)} %copy-done.11, bf16[2048,128]{1,0:T(8,128)(2,1)} %collective-permute-done), kind=kOutput, calls=%fused_computation.47 | convolution fusion | flops 134217728 | bytes 2686976 | tf_op jit(solution)/shard_map/dot_general | solution.py:36
  19.4 1.5 %fusion.3 = f32[2048,256]{0,1:T(8,128)S(1)} fusion(f32[256,2048]{1,0:T(8,128)S(1)} %convolution_add_fusion.4, f32[256,2048]{1,0:T(8,128)S(1)} %fusion.30, bf16[128,256]{1,0:T(8,128)(2,1)S(1)} %copy-done.10, bf16[2048,128]{1,0:T(8,128)(2,1)} %collective-permute-done), kind=kOutput, calls=%fused_computation.9 | convolution fusion | flops 135266304 | bytes 6881280 | tf_op jit(solution)/shard_map/dot_general | solution.py:36
  20.9 0.0 copy-start.9
  20.9 0.5 multiply_subtract_fusion.2
  21.4 0.3 copy-done.9
  21.7 0.5 fusion.17
  22.2 0.0 copy-start.8
  22.2 0.0 copy-start.12
  22.2 0.5 convolution_add_fusion.7
  22.7 0.5 copy-done.8
  23.3 0.5 fusion.5
  23.8 1.0 %copy.32 = bf16[8,256,128]{1,2,0:T(8,128)(2,1)} copy(bf16[8,256,128]{2,1,0:T(8,128)(2,1)S(1)} %bitcast.59) | data formatting | bytes 1048576 | tf_op jit(solution)/shard_map/reshape | solution.py:153
  24.8 11.4 %all-to-all-start = ((bf16[8,256,128]{1,2,0:T(8,128)(2,1)}), bf16[8,256,128]{1,2,0:T(8,128)(2,1)S(1)}, u32[]{:S(2)}, u32[]{:S(2)}) async-start(bf16[8,256,128]{1,2,0:T(8,128)(2,1)} %copy.32), calls=%async_computation | async-start | bytes 1048576 | tf_op jit(solution)/shard_map/all_to_all | solution.py:137
  36.2 1.3 %copy.33 = bf16[256,8,128]{0,2,1:T(8,128)(2,1)S(1)} copy(bf16[256,8,128]{2,0,1:T(8,128)(2,1)} %bitcast.7) | data formatting | bytes 1048576 | tf_op jit(solution)/shard_map/transpose | solution.py:148
  37.5 0.0 slice-start.1
  37.5 4.0 %fusion.34 = f32[2304,256]{0,1:T(8,128)S(1)} fusion(bf16[1024,2304]{1,0:T(8,128)(2,1)} %constant.47.clone, bf16[256,1024]{0,1:T(8,128)(2,1)S(1)} %bitcast.60), kind=kOutput, calls=%fused_computation.51 | convolution fusion | flops 1207959552 | bytes 7602176 | tf_op jit(solution)/shard_map/dot_general | solution.py:36
  41.5 0.0 slice-start.2
  41.5 2.9 %fusion = f32[256,2304]{1,0:T(8,128)} fusion(f32[2304,256]{0,1:T(8,128)S(1)} %fusion.34, bf16[1024,2304]{1,0:T(8,128)(2,1)S(1)} %bitcast.53, bf16[256,1024]{0,1:T(8,128)(2,1)S(1)} %bitcast.61), kind=kOutput, calls=%fused_computation.2 | convolution fusion | flops 1208549376 | bytes 9961472 | tf_op jit(solution)/shard_map/dot_general | solution.py:36
  44.4 7.1 %all-to-all-done = bf16[8,256,128]{1,2,0:T(8,128)(2,1)S(1)} async-done(((bf16[8,256,128]{1,2,0:T(8,128)(2,1)}), bf16[8,256,128]{1,2,0:T(8,128)(2,1)S(1)}, u32[]{:S(2)}, u32[]{:S(2)}) %all-to-all-start) | async-done | bytes 524320 | tf_op jit(solution)/shard_map/all_to_all | solution.py:137
  51.5 3.9 %fusion.33 = f32[256,2304]{1,0:T(8,128)S(1)} fusion(bf16[256,1024]{0,1:T(8,128)(2,1)S(1)} %bitcast.56, bf16[1024,2304]{1,0:T(8,128)(2,1)} %constant.47.clone), kind=kOutput, calls=%fused_computation.50 | convolution fusion | flops 1207959552 | bytes 7602176 | tf_op jit(solution)/shard_map/dot_general | solution.py:36
  55.5 0.0 slice-start.6
  55.5 1.5 %convolution_add_fusion.2 = f32[256,2304]{1,0:T(8,128)S(1)} fusion(f32[256,2304]{1,0:T(8,128)S(1)} %fusion.33, bf16[256,1024]{0,1:T(8,128)(2,1)S(1)} %bitcast.57, bf16[1024,2304]{1,0:T(8,128)(2,1)S(1)} %bitcast.55), kind=kOutput, calls=%fused_computation.3 | convolution fusion | flops 1208549376 | bytes 9961472 | tf_op jit(solution)/shard_map/dot_general | solution.py:36
  57.0 0.1 copy-done.1
  57.1 0.7 copy-done.2
  57.9 0.5 multiply_subtract_fusion
  58.4 0.2 multiply_add_fusion
  58.6 0.5 slice-done.6
  59.1 0.2 slice-done.7
  59.3 1.4 %fusion.13 = f32[256,1024]{1,0:T(8,128)S(1)} fusion(bf16[2304,1024]{1,0:T(8,128)(2,1)S(1)} %bitcast.66, f32[256,1152]{1,0:T(8,128)S(1)} %multiply_add_fusion, f32[256,1152]{1,0:T(8,128)S(1)} %get-tuple-element.5), kind=kOutput, calls=%fused_computation.34 | convolution fusion | flops 1210318848 | bytes 8126464 | tf_op jit(solution)/shard_map/dot_general | solution.py:36
  60.8 0.0 slice-start.5
  60.8 1.4 %convolution_add_fusion.9 = f32[256,1024]{1,0:T(8,128)S(1)} fusion(f32[256,1024]{1,0:T(8,128)S(1)} %fusion.13, bf16[2304,1024]{1,0:T(8,128)(2,1)S(1)} %bitcast.66, f32[256,1152]{1,0:T(8,128)S(1)} %multiply_add_fusion, f32[256,1152]{1,0:T(8,128)S(1)} %get-tuple-element.5), kind=kOutput, calls=%fused_computation.21 | convolution fusion | flops 1211170816 | bytes 9175040 | tf_op jit(solution)/shard_map/dot_general | solution.py:36
  62.2 1.4 %fusion.9 = bf16[32,8,8,128]{3,2,1,0:T(8,128)(2,1)S(1)} fusion(f32[256,1024]{1,0:T(8,128)S(1)} %convolution_add_fusion.9, bf16[2304,1024]{1,0:T(8,128)(2,1)S(1)} %bitcast.64, f32[256,1152]{1,0:T(8,128)S(1)} %multiply_add_fusion, f32[256,1152]{1,0:T(8,128)S(1)} %get-tuple-element.5), kind=kOutput, calls=%fused_computation.23 | convolution fusion | flops 1210843136 | bytes 8650752 | tf_op jit(solution)/shard_map/dot_general | solution.py:36
  63.7 0.1 copy.41
  63.8 17.9 %all_to_all.15 = bf16[8,256,128]{2,1,0:T(8,128)(2,1)S(1)} all-to-all(bf16[8,256,128]{2,1,0:T(8,128)(2,1)S(1)} %bitcast.58), channel_id=1, replica_groups=mesh['grp'=2,'tok'=4,'sec'=2,'ch'=2] {'tok','sec'}, dimensions={0} | all-to-all | bytes 1048576 | tf_op jit(solution)/shard_map/all_to_all | solution.py:137
  81.7 1.0 %fusion.10 = bf16[2048,128]{1,0:T(8,128)(2,1)} fusion(bf16[2048,128]{1,0:T(8,128)(2,1)S(1)} %copy-done.7, bf16[8,256,128]{2,1,0:T(8,128)(2,1)S(1)} %all_to_all.15), kind=kLoop, calls=%fused_computation.30 | loop fusion | flops 1048576 | bytes 1572864 | tf_op jit(solution)/shard_map/convert_element_type | solution.py:164
  (33 shorter events, 0.1 us)
Async XLA Ops:
  0.0 14.3 %copy-start = (bf16[2048,128]{1,0:T(8,128)(2,1)S(1)}, bf16[2048,128]{1,0:T(8,128)(2,1)}, u32[]{:S(2)}) copy-start(bf16[2048,128]{1,0:T(8,128)(2,1)} %param.24) | copy-start | bytes 1572868
  0.0 12.0 %copy-start.13 = (bf16[128,256]{1,0:T(8,128)(2,1)S(1)}, bf16[128,256]{1,0:T(8,128)(2,1)}, u32[]{:S(2)}) copy-start(bf16[128,256]{1,0:T(8,128)(2,1)} %constant.44.clone) | copy-start | bytes 196612
  0.0 12.0 %copy-start.4 = (bf16[2048,128]{1,0:T(8,128)(2,1)S(1)}, bf16[2048,128]{1,0:T(8,128)(2,1)}, u32[]{:S(2)}) copy-start(bf16[2048,128]{1,0:T(8,128)(2,1)} %param.19) | copy-start | bytes 1572868
  0.0 24.8 %all-to-all-start.1 = ((bf16[8,256,128]{2,1,0:T(8,128)(2,1)}), bf16[8,256,128]{2,1,0:T(8,128)(2,1)}, u32[]{:S(2)}, u32[]{:S(2)}) async-start(bf16[8,256,128]{2,1,0:T(8,128)(2,1)} %bitcast.62), calls=%async_computation.1 | async-start | bytes 1048576 | tf_op jit(solution)/shard_map/all_to_all | solution.py:137
  6.5 11.4 %collective-permute-start = (bf16[2048,128]{1,0:T(8,128)(2,1)}, bf16[2048,128]{1,0:T(8,128)(2,1)}, u32[]{:S(2)}, u32[]{:S(2)}) collective-permute-start(bf16[2048,128]{1,0:T(8,128)(2,1)} %param.19), channel_id=1, source_target_pairs={{0,2},{2,4},{4,6},{6,8},{8,10},{10,12},{12,14},{1,3},{3,5},{5,7},{... | collective-permute-start | bytes 1572872 | tf_op jit(solution)/shard_map/ppermute | solution.py:151
  12.0 1.0 %copy-start.3 = (bf16[2048,128]{1,0:T(8,128)(2,1)S(1)}, bf16[2048,128]{1,0:T(8,128)(2,1)}, u32[]{:S(2)}) copy-start(bf16[2048,128]{1,0:T(8,128)(2,1)} %param.21) | copy-start | bytes 1572868
  12.0 1.0 %copy-start.10 = (bf16[128,256]{1,0:T(8,128)(2,1)S(1)}, bf16[128,256]{1,0:T(8,128)(2,1)}, u32[]{:S(2)}) copy-start(bf16[128,256]{1,0:T(8,128)(2,1)} %constant.41.clone) | copy-start | bytes 196612
  13.0 0.8 %copy-start.11 = (bf16[128,256]{1,0:T(8,128)(2,1)S(1)}, bf16[128,256]{1,0:T(8,128)(2,1)}, u32[]{:S(2)}) copy-start(bf16[128,256]{1,0:T(8,128)(2,1)} %constant.42.clone) | copy-start | bytes 196612
  13.9 1.1 %copy-start.5 = (bf16[128,2304]{1,0:T(8,128)(2,1)S(1)}, bf16[128,2304]{1,0:T(8,128)(2,1)}, u32[]{:S(2)}) copy-start(bf16[128,2304]{1,0:T(8,128)(2,1)} %constant.49.clone) | copy-start | bytes 1769476
  14.9 1.1 %copy-start.6 = (bf16[128,2304]{1,0:T(8,128)(2,1)S(1)}, bf16[128,2304]{1,0:T(8,128)(2,1)}, u32[]{:S(2)}) copy-start(bf16[128,2304]{1,0:T(8,128)(2,1)} %constant.50.clone) | copy-start | bytes 1769476
  20.9 0.8 %copy-start.9 = (bf16[256,128]{1,0:T(8,128)(2,1)S(1)}, bf16[256,128]{1,0:T(8,128)(2,1)}, u32[]{:S(2)}) copy-start(bf16[256,128]{1,0:T(8,128)(2,1)} %constant.45.clone) | copy-start | bytes 196612
  22.2 1.0 %copy-start.8 = (bf16[2048,128]{1,0:T(8,128)(2,1)S(1)}, bf16[2048,128]{1,0:T(8,128)(2,1)}, u32[]{:S(2)}) copy-start(bf16[2048,128]{1,0:T(8,128)(2,1)} %param.20) | copy-start | bytes 1572868
  22.2 1.0 %copy-start.12 = (bf16[256,128]{1,0:T(8,128)(2,1)S(1)}, bf16[256,128]{1,0:T(8,128)(2,1)}, u32[]{:S(2)}) copy-start(bf16[256,128]{1,0:T(8,128)(2,1)} %constant.46.clone) | copy-start | bytes 196612
  24.8 26.7 %all-to-all-start = ((bf16[8,256,128]{1,2,0:T(8,128)(2,1)}), bf16[8,256,128]{1,2,0:T(8,128)(2,1)S(1)}, u32[]{:S(2)}, u32[]{:S(2)}) async-start(bf16[8,256,128]{1,2,0:T(8,128)(2,1)} %copy.32), calls=%async_computation | async-start | bytes 1048576 | tf_op jit(solution)/shard_map/all_to_all | solution.py:137
  36.2 5.3 %slice-start = ((s8[4718592]{0:T(1024)(128)(4,1)}), s8[524288]{0:T(1024)(128)(4,1)S(1)}, s32[]{:S(2)}) async-start(s8[4718592]{0:T(1024)(128)(4,1)} %bitcast.52), calls=%async_computation.3 | async-start | bytes 1048576
  37.5 4.0 %slice-start.1 = ((s8[4718592]{0:T(1024)(128)(4,1)}), s8[4194304]{0:T(1024)(128)(4,1)S(1)}, s32[]{:S(2)}) async-start(s8[4718592]{0:T(1024)(128)(4,1)} %bitcast.52), calls=%async_computation.4 | async-start | bytes 8388608
  41.5 14.0 %slice-start.2 = ((s8[4718592]{0:T(1024)(128)(4,1)}), s8[524288]{0:T(1024)(128)(4,1)S(1)}, s32[]{:S(2)}) async-start(s8[4718592]{0:T(1024)(128)(4,1)} %bitcast.54), calls=%async_computation.5 | async-start | bytes 1048576
  51.5 3.9 %slice-start.3 = ((s8[4718592]{0:T(1024)(128)(4,1)}), s8[4194304]{0:T(1024)(128)(4,1)S(1)}, s32[]{:S(2)}) async-start(s8[4718592]{0:T(1024)(128)(4,1)} %bitcast.54), calls=%async_computation.6 | async-start | bytes 8388608
  55.5 1.7 %copy-start.1 = (f32[256,2304]{1,0:T(8,128)S(1)}, f32[256,2304]{1,0:T(8,128)}, u32[]{:S(2)}) copy-start(f32[256,2304]{1,0:T(8,128)} %fusion) | copy-start | bytes 7077892
  55.5 2.4 %copy-start.2 = (f32[256,2304]{1,0:T(8,128)S(1)}, f32[256,2304]{1,0:T(8,128)}, u32[]{:S(2)}) copy-start(f32[256,2304]{1,0:T(8,128)} %convolution_add_fusion) | copy-start | bytes 7077892
  55.5 3.6 %slice-start.6 = ((s8[4718592]{0:T(1024)(128)(4,1)}), s8[4194304]{0:T(1024)(128)(4,1)S(1)}, s32[]{:S(2)}) async-start(s8[4718592]{0:T(1024)(128)(4,1)} %bitcast.65), calls=%async_computation.9 | async-start | bytes 8388608
  57.9 1.5 %slice-start.7 = ((s8[4718592]{0:T(1024)(128)(4,1)}), s8[524288]{0:T(1024)(128)(4,1)S(1)}, s32[]{:S(2)}) async-start(s8[4718592]{0:T(1024)(128)(4,1)} %bitcast.65), calls=%async_computation.10 | async-start | bytes 1048576
  59.3 2.9 %slice-start.4 = ((s8[4718592]{0:T(1024)(128)(4,1)}), s8[4194304]{0:T(1024)(128)(4,1)S(1)}, s32[]{:S(2)}) async-start(s8[4718592]{0:T(1024)(128)(4,1)} %bitcast.63), calls=%async_computation.7 | async-start | bytes 8388608
  60.8 1.5 %slice-start.5 = ((s8[4718592]{0:T(1024)(128)(4,1)}), s8[524288]{0:T(1024)(128)(4,1)S(1)}, s32[]{:S(2)}) async-start(s8[4718592]{0:T(1024)(128)(4,1)} %bitcast.63), calls=%async_computation.8 | async-start | bytes 1048576
  63.7 18.0 %copy-start.7 = (bf16[2048,128]{1,0:T(8,128)(2,1)S(1)}, bf16[2048,128]{1,0:T(8,128)(2,1)}, u32[]{:S(2)}) copy-start(bf16[2048,128]{1,0:T(8,128)(2,1)} %param.25) | copy-start | bytes 1572868

commit v2 on v1

--- a/solution.py
+++ b/solution.py
@@ -5,6 +5,8 @@
 import ml_dtypes
 import numpy as np
 from jax import lax
+from jax.experimental import pallas as pl
+from jax.experimental.pallas import tpu as pltpu
 from jax.sharding import PartitionSpec as P
 
 RING = ("tok", "sec")
@@ -124,13 +126,212 @@
     return result.reshape(channels, seq_len)
 
 
-def dense_pair(signal, filter_rows, skip, taps, half):
-    seq_len = signal.shape[1]
-    table = forward_table(seq_len, half)
-    weights = forward(filter_rows, table)
-    weights = jnp.concatenate([weights[:, :half] + skip, weights[:, half:]], axis=1)
-    weights = times(weights, forward(taps, tuple(piece[: taps.shape[1]] for piece in table)))
-    return backward(times(forward(signal, table), weights), backward_table(seq_len, half))
+def tiled_table(tokens, half):
+    angle = angles(tokens, half).reshape(tokens, half // 128, 1, 128)
+    table = np.concatenate([np.cos(angle), -np.sin(angle)], axis=2)
+    return two_pieces(table.reshape(tokens, 2 * half))
+
+
+def dot_rows(left, right):
+    return lax.dot_general(
+        left, right, (((1,), (1,)), ((), ())), preferred_element_type=jnp.float32
+    )
+
+
+def split(wide):
+    high = wide.astype(jnp.bfloat16)
+    return high, (wide - high.astype(jnp.float32)).astype(jnp.bfloat16)
+
+
+def fused_kernel(
+    features, gate_one, taps_one, long_filter, taps_two, skip, short_high, short_low,
+    table_hbm, table_low, second_conv,
+    table, before, filter_rows, signal, mixed_send, result_send, weights, high, low,
+    table_sem, halo_sems, filter_sent, filter_got, mixed_sent, mixed_got, result_sent, result_got,
+):
+    sections = lax.axis_size("sec")
+    shards = lax.axis_size("tok") * sections
+    me = lax.axis_index("tok") * sections + lax.axis_index("sec")
+    narrow, seq_len = signal.shape
+    length = features.shape[1]
+    tiles = weights.shape[0]
+    half = tiles * 128
+
+    def place(peer):
+        return {"tok": peer // sections, "sec": peer % sections}
+
+    def rows(peer):
+        return pl.ds(pl.multiple_of(peer * narrow, narrow), narrow)
+
+    def tokens(peer):
+        return pl.ds(pl.multiple_of(peer * length, length), length)
+
+    def other(step):
+        return lax.rem(me + step, shards)
+
+    def remote(source, target, sent, got, peer):
+        return pltpu.make_async_remote_copy(
+            src_ref=source, dst_ref=target, send_sem=sent, recv_sem=got,
+            device_id=place(peer), device_id_type=pl.DeviceIdType.MESH,
+        )
+
+    load = pltpu.make_async_copy(table_hbm, table, table_sem)
+    load.start()
+    barrier = pltpu.get_barrier_semaphore()
+    for step in range(1, shards):
+        pl.semaphore_signal(
+            barrier, inc=1, device_id=place(other(step)), device_id_type=pl.DeviceIdType.MESH
+        )
+    pl.semaphore_wait(barrier, shards - 1)
+
+    halo = remote(features, before, halo_sems.at[0], halo_sems.at[1], other(1))
+
+    @pl.when(me < shards - 1)
+    def _():
+        halo.start()
+
+    def filter_copy(peer, slot):
+        return remote(
+            long_filter.at[rows(peer)], filter_rows.at[:, tokens(slot)],
+            filter_sent.at[peer], filter_got.at[slot], peer,
+        )
+
+    def mixed_copy(peer, slot):
+        return remote(
+            mixed_send.at[peer], signal.at[:, tokens(slot)],
+            mixed_sent.at[peer], mixed_got.at[slot], peer,
+        )
+
+    def result_copy(peer, slot):
+        return remote(
+            result_send.at[peer], second_conv.at[rows(slot)],
+            result_sent.at[peer], result_got.at[slot], peer,
+        )
+
+    for step in range(1, shards):
+        filter_copy(other(step), me).start()
+    filter_rows[:, tokens(me)] = long_filter[rows(me)]
+
+    @pl.when(me == 0)
+    def _():
+        before[...] = jnp.zeros_like(before)
+
+    @pl.when(me > 0)
+    def _():
+        halo.wait_recv()
+
+    early = (short_high[:length], short_low[:length])
+    late = (short_high[length:], short_low[length:])
+
+    def first_conv(peer):
+        part = rows(peer)
+        spectrum = forward(before[part], early) + forward(features[part], late)
+        x_high, x_low = split(times(spectrum, forward(taps_one[part], early)))
+        conv = dot_rows(x_high, late[0]) + dot_rows(x_low, late[0]) + dot_rows(x_high, late[1])
+        return (conv * (1.0 / length) * gate_one[part].astype(jnp.float32)).astype(jnp.bfloat16)
+
+    @pl.loop(1, shards)
+    def _(step):
+        peer = other(step)
+        mixed_send[peer] = first_conv(peer)
+        mixed_copy(peer, me).start()
+
+    signal[:, tokens(me)] = first_conv(me)
+
+    load.wait()
+    for step in range(1, shards):
+        filter_copy(other(step), other(step)).wait_recv()
+
+    def columns(tile):
+        return pl.ds(pl.multiple_of(tile * 256, 256), 256)
+
+    gain = skip[...]
+    taps = taps_two[rows(me)]
+
+    @pl.loop(0, tiles)
+    def _(tile):
+        own = columns(tile)
+        spectrum = dot(filter_rows[...], table[:, own])
+        spectrum = jnp.concatenate([spectrum[:, :128] + gain, spectrum[:, 128:]], axis=1)
+        short = dot(taps, table[:length, own]) + dot(taps, table_low[:, own])
+        weights[tile] = times(spectrum, short) * (1.0 / half)
+
+    for step in range(1, shards):
+        mixed_copy(other(step), other(step)).wait_recv()
+
+    @pl.loop(0, tiles)
+    def _(tile):
+        own = columns(tile)
+        x_high, x_low = split(times(dot(signal[...], table[:, own]), weights[tile]))
+        high[:, own] = x_high
+        low[:, own] = x_low
+
+    width = sections * length
+    groups = shards // sections
+
+    @pl.loop(1, groups + 1)
+    def _(step):
+        group = lax.rem(lax.axis_index("tok") + step, groups)
+        part = table[pl.ds(pl.multiple_of(group * width, width), width)]
+        result = (dot_rows(high[...], part) + dot_rows(low[...], part)).astype(jnp.bfloat16)
+        for section in range(sections):
+            peer = group * sections + section
+            block = result[:, section * length : (section + 1) * length]
+
+            @pl.when(peer != me)
+            def _():
+                result_send[peer] = block
+                result_copy(peer, me).start()
+
+            @pl.when(peer == me)
+            def _():
+                second_conv[rows(me)] = block
+
+    for step in range(1, shards):
+        result_copy(other(step), other(step)).wait_recv()
+    for step in range(1, shards):
+        filter_copy(other(step), me).wait_send()
+        mixed_copy(other(step), me).wait_send()
+        result_copy(other(step), me).wait_send()
+
+    @pl.when(me < shards - 1)
+    def _():
+        halo.wait_send()
+
+
+def fused(features, gate_one, taps_one, long_filter, taps_two, skip, shards, half):
+    channels, length = features.shape
+    narrow = channels // shards
+    seq_len = shards * length
+    table, table_low = tiled_table(seq_len, half)
+    short_high, short_low = forward_table(2 * length, length)
+    vmem = pl.BlockSpec(memory_space=pltpu.VMEM)
+    half_type = jnp.bfloat16
+    peers = pltpu.SemaphoreType.DMA((shards,))
+    return pl.pallas_call(
+        fused_kernel,
+        out_shape=jax.ShapeDtypeStruct((channels, length), half_type),
+        in_specs=[vmem] * 8 + [pl.BlockSpec(memory_space=pl.ANY), vmem],
+        out_specs=vmem,
+        scratch_shapes=[
+            pltpu.VMEM((seq_len, 2 * half), half_type),
+            pltpu.VMEM((channels, length), half_type),
+            pltpu.VMEM((narrow, seq_len), half_type),
+            pltpu.VMEM((narrow, seq_len), half_type),
+            pltpu.VMEM((shards, narrow, length), half_type),
+            pltpu.VMEM((shards, narrow, length), half_type),
+            pltpu.VMEM((half // 128, narrow, 256), jnp.float32),
+            pltpu.VMEM((narrow, 2 * half), half_type),
+            pltpu.VMEM((narrow, 2 * half), half_type),
+            pltpu.SemaphoreType.DMA,
+            pltpu.SemaphoreType.DMA((2,)),
+            peers, peers, peers, peers, peers, peers,
+        ],
+        compiler_params=pltpu.CompilerParams(
+            collective_id=0, has_side_effects=True, vmem_limit_bytes=40 * 1024 * 1024
+        ),
+    )(features, gate_one, taps_one, long_filter, taps_two, skip, short_high, short_low,
+      table, table_low[:length])
 
 
 def exchange(blocks):
@@ -144,6 +345,15 @@
     seq_len = block_len * shards
     length = taps_one.shape[1]
 
+    first = lax.axis_index(RING) * narrow
+    skip = lax.dynamic_slice_in_dim(skip_gain, first, narrow)[:, None]
+    half = -(-(2 * seq_len + length) // 256) * 128
+    if seq_len * half <= TABLE_LIMIT:
+        second_conv = fused(
+            features, gate_one, taps_one, long_filter, taps_two, skip, shards, half
+        )
+        return (second_conv.astype(jnp.float32) * gate_two).astype(jnp.bfloat16)
+
     def rows_of(blocks):
         return jnp.swapaxes(blocks, 0, 1).reshape(narrow, seq_len)
 
@@ -151,14 +361,8 @@
     before = lax.ppermute(features, RING, [(i, i + 1) for i in range(shards - 1)])
     mixed_one = (short_conv(before, features, taps_one) * gate_one).astype(jnp.bfloat16)
     signal = rows_of(exchange(mixed_one.reshape(shards, narrow, block_len)))
-    first = lax.axis_index(RING) * narrow
-    skip = lax.dynamic_slice_in_dim(skip_gain, first, narrow)[:, None]
     taps = lax.dynamic_slice_in_dim(taps_two, first, narrow)
-    half = -(-(2 * seq_len + length) // 256) * 128
-    if seq_len * half <= TABLE_LIMIT:
-        result = dense_pair(signal, filter_rows, skip, taps, half)
-    else:
-        result = factored_pair(signal, filter_rows, skip, taps)
+    result = factored_pair(signal, filter_rows, skip, taps)
     result = result.astype(jnp.bfloat16).reshape(narrow, shards, block_len)
     second_conv = exchange(jnp.swapaxes(result, 0, 1)).reshape(channels, block_len)
     return (second_conv.astype(jnp.float32) * gate_two).astype(jnp.bfloat16)

time: 83.4 us -> 60.8 us (0.73)
  the two profiles are of different devices: /device:TPU:0 before, /device:TPU:9 now
where the time goes in v2:
time: 60.8 us; the launch traced here: 60.3 us
  Pallas kernels  48 us (79%)
  local copies, waits for them, and re-layouts  11.3 us (19%)
  other arithmetic  0.93 us (2%)
    pallas_call x1, Pallas kernels, fused(): pl.pallas_call(fused_kernel, out_shape=jax.ShapeDtypeStruct((channels, le...  48 us
    unnamed x20, local copies, waits for them, and re-layouts  10.4 us

profile of v2, /device:TPU:9, one launch (start us, length us, event | category | flops | bytes accessed | tf_op | source)
XLA Modules:
  0.0 60.3 jit_solution(13066562492171277089)
XLA Ops:
  0.0 0.8 %dynamic_slice.3 = f32[256]{0:T(256)S(1)} dynamic-slice(f32[2048]{0:T(1024)} %param.15, s32[]{:T(128)S(6)} %select_n.3), dynamic_slice_sizes={256} | dynamic-slice | bytes 2052 | tf_op jit(solution)/shard_map/dynamic_slice | solution.py:349
  0.8 0.1 copy.12.skip
  0.9 0.0 copy-start
  0.9 2.3 %copy-done = bf16[1024,2304]{1,0:T(8,128)(2,1)S(1)} copy-done((bf16[1024,2304]{1,0:T(8,128)(2,1)S(1)}, bf16[1024,2304]{1,0:T(8,128)(2,1)}, u32[]{:S(2)}) %copy-start) | copy-done | bytes 4718616
  3.2 0.0 copy-start.1
  3.2 1.1 %copy-done.1 = bf16[128,2304]{1,0:T(8,128)(2,1)S(1)} copy-done((bf16[128,2304]{1,0:T(8,128)(2,1)S(1)}, bf16[128,2304]{1,0:T(8,128)(2,1)}, u32[]{:S(2)}) %copy-start.1) | copy-done | bytes 589848
  4.3 0.0 copy-start.2
  4.3 1.0 %copy-done.2 = bf16[2048,128]{1,0:T(8,128)(2,1)S(1)} copy-done((bf16[2048,128]{1,0:T(8,128)(2,1)S(1)}, bf16[2048,128]{1,0:T(8,128)(2,1)}, u32[]{:S(2)}) %copy-start.2) | copy-done | bytes 524312
  5.4 0.0 copy-start.3
  5.4 1.0 %copy-done.3 = bf16[2048,128]{1,0:T(8,128)(2,1)S(1)} copy-done((bf16[2048,128]{1,0:T(8,128)(2,1)S(1)}, bf16[2048,128]{1,0:T(8,128)(2,1)}, u32[]{:S(2)}) %copy-start.3) | copy-done | bytes 524312
  6.4 0.0 copy-start.4
  6.4 1.0 %copy-done.4 = bf16[2048,128]{1,0:T(8,128)(2,1)S(1)} copy-done((bf16[2048,128]{1,0:T(8,128)(2,1)S(1)}, bf16[2048,128]{1,0:T(8,128)(2,1)}, u32[]{:S(2)}) %copy-start.4) | copy-done | bytes 524312
  7.4 0.0 copy-start.5
  7.4 1.0 %copy-done.5 = bf16[2048,128]{1,0:T(8,128)(2,1)S(1)} copy-done((bf16[2048,128]{1,0:T(8,128)(2,1)S(1)}, bf16[2048,128]{1,0:T(8,128)(2,1)}, u32[]{:S(2)}) %copy-start.5) | copy-done | bytes 524312
  8.5 0.0 copy-start.6
  8.5 1.0 %copy-done.6 = bf16[2048,128]{1,0:T(8,128)(2,1)S(1)} copy-done((bf16[2048,128]{1,0:T(8,128)(2,1)S(1)}, bf16[2048,128]{1,0:T(8,128)(2,1)}, u32[]{:S(2)}) %copy-start.6) | copy-done | bytes 524312
  9.5 0.0 copy-start.7
  9.5 0.9 %copy-done.7 = bf16[256,256]{1,0:T(8,128)(2,1)S(1)} copy-done((bf16[256,256]{1,0:T(8,128)(2,1)S(1)}, bf16[256,256]{1,0:T(8,128)(2,1)}, u32[]{:S(2)}) %copy-start.7) | copy-done | bytes 131096
  10.4 0.0 copy-start.8
  10.4 0.9 %copy-done.8 = bf16[256,256]{1,0:T(8,128)(2,1)S(1)} copy-done((bf16[256,256]{1,0:T(8,128)(2,1)S(1)}, bf16[256,256]{1,0:T(8,128)(2,1)}, u32[]{:S(2)}) %copy-start.8) | copy-done | bytes 131096
  11.3 0.0 copy-start.9
  11.3 48.0 %shard_map.109 = bf16[2048,128]{1,0:T(8,128)(2,1)S(1)} custom-call(bf16[2048,128]{1,0:T(8,128)(2,1)S(1)} %copy-done.2, bf16[2048,128]{1,0:T(8,128)(2,1)S(1)} %copy-done.3, bf16[2048,128]{1,0:T(8,128)(2,1)S(1)} %copy-done.4, bf16[2048,128]{1,0:T(8,128)(2,1)S(1)} %copy-done.5, bf16[2048,128]{1,0:T(8,128)(2,1)S(1)} %copy-done.6, f32[256,1]{1,0:T(8,128)S(1)} %copy.12.skip, ...), custom_call_target="tpu_custom_call" | custom-call | tf_op jit(solution)/shard_map/pallas_call | solution.py:311
  59.4 0.0 copy-done.9
  59.4 0.9 %multiply_convert_fusion = bf16[2048,128]{1,0:T(8,128)(2,1)} fusion(bf16[2048,128]{1,0:T(8,128)(2,1)S(1)} %copy-done.9, bf16[2048,128]{1,0:T(8,128)(2,1)S(1)} %shard_map.109), kind=kLoop, calls=%fused_computation | loop fusion | flops 1048576 | bytes 1572864 | tf_op jit(solution)/shard_map/convert_element_type | solution.py:355
Async XLA Ops:
  0.9 2.3 %copy-start = (bf16[1024,2304]{1,0:T(8,128)(2,1)S(1)}, bf16[1024,2304]{1,0:T(8,128)(2,1)}, u32[]{:S(2)}) copy-start(bf16[1024,2304]{1,0:T(8,128)(2,1)} %constant.27.clone.table_hbm) | copy-start | bytes 14155780
  3.2 1.1 %copy-start.1 = (bf16[128,2304]{1,0:T(8,128)(2,1)S(1)}, bf16[128,2304]{1,0:T(8,128)(2,1)}, u32[]{:S(2)}) copy-start(bf16[128,2304]{1,0:T(8,128)(2,1)} %constant.28.clone.table_low) | copy-start | bytes 1769476
  4.3 1.0 %copy-start.2 = (bf16[2048,128]{1,0:T(8,128)(2,1)S(1)}, bf16[2048,128]{1,0:T(8,128)(2,1)}, u32[]{:S(2)}) copy-start(bf16[2048,128]{1,0:T(8,128)(2,1)} %features.1) | copy-start | bytes 1572868
  5.4 1.0 %copy-start.3 = (bf16[2048,128]{1,0:T(8,128)(2,1)S(1)}, bf16[2048,128]{1,0:T(8,128)(2,1)}, u32[]{:S(2)}) copy-start(bf16[2048,128]{1,0:T(8,128)(2,1)} %gate_one.1) | copy-start | bytes 1572868
  6.4 1.0 %copy-start.4 = (bf16[2048,128]{1,0:T(8,128)(2,1)S(1)}, bf16[2048,128]{1,0:T(8,128)(2,1)}, u32[]{:S(2)}) copy-start(bf16[2048,128]{1,0:T(8,128)(2,1)} %taps_one.1) | copy-start | bytes 1572868
  7.4 1.0 %copy-start.5 = (bf16[2048,128]{1,0:T(8,128)(2,1)S(1)}, bf16[2048,128]{1,0:T(8,128)(2,1)}, u32[]{:S(2)}) copy-start(bf16[2048,128]{1,0:T(8,128)(2,1)} %long_filter.1) | copy-start | bytes 1572868
  8.5 1.0 %copy-start.6 = (bf16[2048,128]{1,0:T(8,128)(2,1)S(1)}, bf16[2048,128]{1,0:T(8,128)(2,1)}, u32[]{:S(2)}) copy-start(bf16[2048,128]{1,0:T(8,128)(2,1)} %taps_two.1) | copy-start | bytes 1572868
  9.5 0.9 %copy-start.7 = (bf16[256,256]{1,0:T(8,128)(2,1)S(1)}, bf16[256,256]{1,0:T(8,128)(2,1)}, u32[]{:S(2)}) copy-start(bf16[256,256]{1,0:T(8,128)(2,1)} %constant.26.clone.short_low) | copy-start | bytes 393220
  10.4 0.9 %copy-start.8 = (bf16[256,256]{1,0:T(8,128)(2,1)S(1)}, bf16[256,256]{1,0:T(8,128)(2,1)}, u32[]{:S(2)}) copy-start(bf16[256,256]{1,0:T(8,128)(2,1)} %constant.25.clone.short_high) | copy-start | bytes 393220
  11.3 48.0 %copy-start.9 = (bf16[2048,128]{1,0:T(8,128)(2,1)S(1)}, bf16[2048,128]{1,0:T(8,128)(2,1)}, u32[]{:S(2)}) copy-start(bf16[2048,128]{1,0:T(8,128)(2,1)} %param.17) | copy-start | bytes 1572868

commit v3 on v2

--- a/solution.py
+++ b/solution.py
@@ -144,10 +144,11 @@
 
 
 def fused_kernel(
-    features, gate_one, taps_one, long_filter, taps_two, skip, short_high, short_low,
-    table_hbm, table_low, second_conv,
-    table, before, filter_rows, signal, mixed_send, result_send, weights, high, low,
-    table_sem, halo_sems, filter_sent, filter_got, mixed_sent, mixed_got, result_sent, result_got,
+    features_hbm, gate_hbm, taps_hbm, long_filter, taps_two, short_high_hbm, short_low_hbm,
+    table_hbm, table_low_hbm, skip, second_conv,
+    features, gate_one, taps_one, own_taps, short_high, short_low, table_low,
+    table, before, filter_rows, signal, mixed_send, result_send, weights, high,
+    load_sems, halo_sems, filter_sent, filter_got, mixed_sent, mixed_got, result_sent, result_got,
 ):
     sections = lax.axis_size("sec")
     shards = lax.axis_size("tok") * sections
@@ -175,8 +176,18 @@
             device_id=place(peer), device_id_type=pl.DeviceIdType.MESH,
         )
 
-    load = pltpu.make_async_copy(table_hbm, table, table_sem)
-    load.start()
+    pairs = (
+        (features_hbm, features), (taps_hbm, taps_one), (short_high_hbm, short_high),
+        (short_low_hbm, short_low), (gate_hbm, gate_one),
+        (long_filter.at[rows(me)], filter_rows.at[:, tokens(me)]),
+        (taps_two.at[rows(me)], own_taps), (table_low_hbm, table_low), (table_hbm, table),
+    )
+    loads = [
+        pltpu.make_async_copy(source, target, load_sems.at[index])
+        for index, (source, target) in enumerate(pairs)
+    ]
+    for load in loads:
+        load.start()
     barrier = pltpu.get_barrier_semaphore()
     for step in range(1, shards):
         pl.semaphore_signal(
@@ -184,7 +195,7 @@
         )
     pl.semaphore_wait(barrier, shards - 1)
 
-    halo = remote(features, before, halo_sems.at[0], halo_sems.at[1], other(1))
+    halo = remote(features_hbm, before, halo_sems.at[0], halo_sems.at[1], other(1))
 
     @pl.when(me < shards - 1)
     def _():
@@ -210,7 +221,6 @@
 
     for step in range(1, shards):
         filter_copy(other(step), me).start()
-    filter_rows[:, tokens(me)] = long_filter[rows(me)]
 
     @pl.when(me == 0)
     def _():
@@ -220,6 +230,8 @@
     def _():
         halo.wait_recv()
 
+    for load in loads[:5]:
+        load.wait()
     early = (short_high[:length], short_low[:length])
     late = (short_high[length:], short_low[length:])
 
@@ -238,7 +250,8 @@
 
     signal[:, tokens(me)] = first_conv(me)
 
-    load.wait()
+    for load in loads[5:]:
+        load.wait()
     for step in range(1, shards):
         filter_copy(other(step), other(step)).wait_recv()
 
@@ -246,7 +259,7 @@
         return pl.ds(pl.multiple_of(tile * 256, 256), 256)
 
     gain = skip[...]
-    taps = taps_two[rows(me)]
+    taps = own_taps[...]
 
     @pl.loop(0, tiles)
     def _(tile):
@@ -262,9 +275,8 @@
     @pl.loop(0, tiles)
     def _(tile):
         own = columns(tile)
-        x_high, x_low = split(times(dot(signal[...], table[:, own]), weights[tile]))
-        high[:, own] = x_high
-        low[:, own] = x_low
+        product = times(dot(signal[...], table[:, own]), weights[tile])
+        high[:, own] = product.astype(jnp.bfloat16)
 
     width = sections * length
     groups = shards // sections
@@ -273,7 +285,7 @@
     def _(step):
         group = lax.rem(lax.axis_index("tok") + step, groups)
         part = table[pl.ds(pl.multiple_of(group * width, width), width)]
-        result = (dot_rows(high[...], part) + dot_rows(low[...], part)).astype(jnp.bfloat16)
+        result = dot_rows(high[...], part).astype(jnp.bfloat16)
         for section in range(sections):
             peer = group * sections + section
             block = result[:, section * length : (section + 1) * length]
@@ -311,9 +323,16 @@
     return pl.pallas_call(
         fused_kernel,
         out_shape=jax.ShapeDtypeStruct((channels, length), half_type),
-        in_specs=[vmem] * 8 + [pl.BlockSpec(memory_space=pl.ANY), vmem],
+        in_specs=[pl.BlockSpec(memory_space=pl.ANY)] * 9 + [vmem],
         out_specs=vmem,
         scratch_shapes=[
+            pltpu.VMEM((channels, length), half_type),
+            pltpu.VMEM((channels, length), half_type),
+            pltpu.VMEM((channels, length), half_type),
+            pltpu.VMEM((narrow, length), half_type),
+            pltpu.VMEM((2 * length, 2 * length), half_type),
+            pltpu.VMEM((2 * length, 2 * length), half_type),
+            pltpu.VMEM((length, 2 * half), half_type),
             pltpu.VMEM((seq_len, 2 * half), half_type),
             pltpu.VMEM((channels, length), half_type),
             pltpu.VMEM((narrow, seq_len), half_type),
@@ -322,16 +341,15 @@
             pltpu.VMEM((shards, narrow, length), half_type),
             pltpu.VMEM((half // 128, narrow, 256), jnp.float32),
             pltpu.VMEM((narrow, 2 * half), half_type),
-            pltpu.VMEM((narrow, 2 * half), half_type),
-            pltpu.SemaphoreType.DMA,
+            pltpu.SemaphoreType.DMA((9,)),
             pltpu.SemaphoreType.DMA((2,)),
             peers, peers, peers, peers, peers, peers,
         ],
         compiler_params=pltpu.CompilerParams(
-            collective_id=0, has_side_effects=True, vmem_limit_bytes=40 * 1024 * 1024
+            collective_id=0, has_side_effects=True, vmem_limit_bytes=56 * 1024 * 1024
         ),
-    )(features, gate_one, taps_one, long_filter, taps_two, skip, short_high, short_low,
-      table, table_low[:length])
+    )(features, gate_one, taps_one, long_filter, taps_two, short_high, short_low,
+      table, table_low[:length], skip)
 
 
 def exchange(blocks):

time: 60.8 us -> 52.7 us (0.87)
  local copies, waits for them, and re-layouts: 11.3 us -> 1.62 us
  other arithmetic: 0.93 us -> 1.97 us
  Pallas kernels: 48 us -> 48.9 us
    unnamed x20 -> x2, local copies, waits for them, and re-layouts: 10.4 us -> 0.01 us
    convert_element_type x1, other arithmetic: 0.93 us -> 1.97 us  [on_device(): return (second_conv.astype(jnp.float32) * gate_two).astype(jnp.bfloat16)]
    pallas_call x1, Pallas kernels: 48 us -> 48.9 us  [fused(): pl.pallas_call(fused_kernel, out_shape=jax.ShapeDtypeStruct((channels, le...]
    broadcast_in_dim x1, local copies, waits for them, and re-layouts: 0.13 us -> 0.8 us  [on_device(): skip = lax.dynamic_slice_in_dim(skip_gain, first, narrow)[:, None]]
where the time goes in v3:
time: 52.7 us; the launch traced here: 52.6 us
  Pallas kernels  48.9 us (93%)
  other arithmetic  1.97 us (4%)
  local copies, waits for them, and re-layouts  1.62 us (3%)
    pallas_call x1, Pallas kernels, fused(): pl.pallas_call(fused_kernel, out_shape=jax.ShapeDtypeStruct((channels, le...  48.9 us
    convert_element_type x1, other arithmetic, on_device(): return (second_conv.astype(jnp.float32) * gate_two).astype(jnp.bfloat16)  1.97 us

profile of v3, /device:TPU:9, one launch (start us, length us, event | category | flops | bytes accessed | tf_op | source)
XLA Modules:
  0.0 52.6 jit_solution(6096781222883465041)
XLA Ops:
  0.0 0.0 copy-start
  0.0 0.8 %dynamic_slice.3 = f32[256]{0:T(256)S(1)} dynamic-slice(f32[2048]{0:T(1024)} %param.15, s32[]{:T(128)S(6)} %select_n.3), dynamic_slice_sizes={256} | dynamic-slice | bytes 2052 | tf_op jit(solution)/shard_map/dynamic_slice | solution.py:367
  0.8 0.8 %copy.12.skip = f32[256,1]{1,0:T(8,128)} copy(f32[256,1]{0,1:T(1,128)S(1)} %bitcast.1) | data formatting | bytes 2048 | tf_op jit(solution)/shard_map/broadcast_in_dim | solution.py:367
  1.6 48.9 %shard_map.109 = bf16[2048,128]{1,0:T(8,128)(2,1)} custom-call(bf16[2048,128]{1,0:T(8,128)(2,1)} %features_hbm.1, bf16[2048,128]{1,0:T(8,128)(2,1)} %gate_hbm.1, bf16[2048,128]{1,0:T(8,128)(2,1)} %taps_hbm.1, bf16[2048,128]{1,0:T(8,128)(2,1)} %long_filter.1, bf16[2048,128]{1,0:T(8,128)(2,1)} %taps_two.1, bf16[256,256]{1,0:T(8,128)(2,1)} %constant.25.clone.short_high_hbm, ...), custom_call_target="tpu_custom_call" | custom-call | tf_op jit(solution)/shard_map/pallas_call | solution.py:323
  50.6 0.0 copy-done
  50.6 2.0 %multiply_convert_fusion = bf16[2048,128]{1,0:T(8,128)(2,1)} fusion(bf16[2048,128]{1,0:T(8,128)(2,1)S(1)} %copy-done, bf16[2048,128]{1,0:T(8,128)(2,1)} %shard_map.109), kind=kLoop, calls=%fused_computation | loop fusion | flops 1048576 | bytes 1572864 | tf_op jit(solution)/shard_map/convert_element_type | solution.py:373
Async XLA Ops:
  0.0 50.6 %copy-start = (bf16[2048,128]{1,0:T(8,128)(2,1)S(1)}, bf16[2048,128]{1,0:T(8,128)(2,1)}, u32[]{:S(2)}) copy-start(bf16[2048,128]{1,0:T(8,128)(2,1)} %param.17) | copy-start | bytes 1572868

commit v4 on v3

--- a/solution.py
+++ b/solution.py
@@ -149,6 +149,7 @@
     features, gate_one, taps_one, own_taps, short_high, short_low, table_low,
     table, before, filter_rows, signal, mixed_send, result_send, weights, high,
     load_sems, halo_sems, filter_sent, filter_got, mixed_sent, mixed_got, result_sent, result_got,
+    relay_sent, relay_got,
 ):
     sections = lax.axis_size("sec")
     shards = lax.axis_size("tok") * sections
@@ -157,6 +158,12 @@
     length = features.shape[1]
     tiles = weights.shape[0]
     half = tiles * 128
+    copies = lax.axis_size("grp")
+    mine = lax.axis_index("grp")
+    share = narrow // copies
+
+    def share_rows(start, owner):
+        return pl.ds(pl.multiple_of(start * narrow + owner * share, share), share)
 
     def place(peer):
         return {"tok": peer // sections, "sec": peer % sections}
@@ -179,7 +186,7 @@
     pairs = (
         (features_hbm, features), (taps_hbm, taps_one), (short_high_hbm, short_high),
         (short_low_hbm, short_low), (gate_hbm, gate_one),
-        (long_filter.at[rows(me)], filter_rows.at[:, tokens(me)]),
+        (long_filter.at[share_rows(me, mine)], filter_rows.at[share_rows(0, mine), tokens(me)]),
         (taps_two.at[rows(me)], own_taps), (table_low_hbm, table_low), (table_hbm, table),
     )
     loads = [
@@ -193,7 +200,12 @@
         pl.semaphore_signal(
             barrier, inc=1, device_id=place(other(step)), device_id_type=pl.DeviceIdType.MESH
         )
-    pl.semaphore_wait(barrier, shards - 1)
+    for step in range(1, copies):
+        pl.semaphore_signal(
+            barrier, inc=1, device_id={"grp": lax.rem(mine + step, copies)},
+            device_id_type=pl.DeviceIdType.MESH,
+        )
+    pl.semaphore_wait(barrier, shards + copies - 2)
 
     halo = remote(features_hbm, before, halo_sems.at[0], halo_sems.at[1], other(1))
 
@@ -203,8 +215,15 @@
 
     def filter_copy(peer, slot):
         return remote(
-            long_filter.at[rows(peer)], filter_rows.at[:, tokens(slot)],
+            long_filter.at[share_rows(peer, mine)], filter_rows.at[share_rows(0, mine), tokens(slot)],
             filter_sent.at[peer], filter_got.at[slot], peer,
+        )
+
+    def relay_copy(peer, owner):
+        part = filter_rows.at[share_rows(0, owner)]
+        return pltpu.make_async_remote_copy(
+            src_ref=part, dst_ref=part, send_sem=relay_sent.at[peer], recv_sem=relay_got.at[owner],
+            device_id={"grp": peer}, device_id_type=pl.DeviceIdType.MESH,
         )
 
     def mixed_copy(peer, slot):
@@ -254,6 +273,11 @@
         load.wait()
     for step in range(1, shards):
         filter_copy(other(step), other(step)).wait_recv()
+    partners = [lax.rem(mine + step, copies) for step in range(1, copies)]
+    for partner in partners:
+        relay_copy(partner, mine).start()
+    for partner in partners:
+        relay_copy(partner, partner).wait_recv()
 
     def columns(tile):
         return pl.ds(pl.multiple_of(tile * 256, 256), 256)
@@ -305,6 +329,8 @@
         filter_copy(other(step), me).wait_send()
         mixed_copy(other(step), me).wait_send()
         result_copy(other(step), me).wait_send()
+    for partner in partners:
+        relay_copy(partner, mine).wait_send()
 
     @pl.when(me < shards - 1)
     def _():
@@ -312,6 +338,7 @@
 
 
 def fused(features, gate_one, taps_one, long_filter, taps_two, skip, shards, half):
+    copies = lax.axis_size("grp")
     channels, length = features.shape
     narrow = channels // shards
     seq_len = shards * length
@@ -344,6 +371,7 @@
             pltpu.SemaphoreType.DMA((9,)),
             pltpu.SemaphoreType.DMA((2,)),
             peers, peers, peers, peers, peers, peers,
+            pltpu.SemaphoreType.DMA((copies,)), pltpu.SemaphoreType.DMA((copies,)),
         ],
         compiler_params=pltpu.CompilerParams(
             collective_id=0, has_side_effects=True, vmem_limit_bytes=56 * 1024 * 1024

time: 52.7 us -> 53.1 us (level)
  no operation moved by 1% of the time
where the time goes in v4:
time: 53.1 us; the launch traced here: 52.5 us
  Pallas kernels  48.9 us (92%)
  other arithmetic  1.97 us (4%)
  local copies, waits for them, and re-layouts  1.62 us (3%)
    pallas_call x1, Pallas kernels, fused(): pl.pallas_call(fused_kernel, out_shape=jax.ShapeDtypeStruct((channels, le...  48.9 us
    convert_element_type x1, other arithmetic, on_device(): return (second_conv.astype(jnp.float32) * gate_two).astype(jnp.bfloat16)  1.97 us

profile of v4, /device:TPU:9, one launch (start us, length us, event | category | flops | bytes accessed | tf_op | source)
XLA Modules:
  0.0 52.5 jit_solution(10078819996714381554)
XLA Ops:
  0.0 0.0 copy-start
  0.0 0.8 %dynamic_slice.3 = f32[256]{0:T(256)S(1)} dynamic-slice(f32[2048]{0:T(1024)} %param.15, s32[]{:T(128)S(6)} %select_n.3), dynamic_slice_sizes={256} | dynamic-slice | bytes 2052 | tf_op jit(solution)/shard_map/dynamic_slice | solution.py:395
  0.8 0.8 %copy.12.skip = f32[256,1]{1,0:T(8,128)} copy(f32[256,1]{0,1:T(1,128)S(1)} %bitcast.1) | data formatting | bytes 2048 | tf_op jit(solution)/shard_map/broadcast_in_dim | solution.py:395
  1.6 48.9 %shard_map.109 = bf16[2048,128]{1,0:T(8,128)(2,1)} custom-call(bf16[2048,128]{1,0:T(8,128)(2,1)} %features_hbm.1, bf16[2048,128]{1,0:T(8,128)(2,1)} %gate_hbm.1, bf16[2048,128]{1,0:T(8,128)(2,1)} %taps_hbm.1, bf16[2048,128]{1,0:T(8,128)(2,1)} %long_filter.1, bf16[2048,128]{1,0:T(8,128)(2,1)} %taps_two.1, bf16[256,256]{1,0:T(8,128)(2,1)} %constant.25.clone.short_high_hbm, ...), custom_call_target="tpu_custom_call" | custom-call | tf_op jit(solution)/shard_map/pallas_call | solution.py:350
  50.5 0.0 copy-done
  50.5 2.0 %multiply_convert_fusion = bf16[2048,128]{1,0:T(8,128)(2,1)} fusion(bf16[2048,128]{1,0:T(8,128)(2,1)S(1)} %copy-done, bf16[2048,128]{1,0:T(8,128)(2,1)} %shard_map.109), kind=kLoop, calls=%fused_computation | loop fusion | flops 1048576 | bytes 1572864 | tf_op jit(solution)/shard_map/convert_element_type | solution.py:401
Async XLA Ops:
  0.0 50.5 %copy-start = (bf16[2048,128]{1,0:T(8,128)(2,1)S(1)}, bf16[2048,128]{1,0:T(8,128)(2,1)}, u32[]{:S(2)}) copy-start(bf16[2048,128]{1,0:T(8,128)(2,1)} %param.17) | copy-start | bytes 1572868

commit v5 on v4

--- a/solution.py
+++ b/solution.py
@@ -238,8 +238,6 @@
             result_sent.at[peer], result_got.at[slot], peer,
         )
 
-    for step in range(1, shards):
-        filter_copy(other(step), me).start()
 
     @pl.when(me == 0)
     def _():
@@ -248,6 +246,9 @@
     @pl.when(me > 0)
     def _():
         halo.wait_recv()
+
+    for step in range(1, shards):
+        filter_copy(other(step), me).start()
 
     for load in loads[:5]:
         load.wait()

time: 53.1 us -> 55.2 us (1.040)
  Pallas kernels: 48.9 us -> 51.4 us
    pallas_call x1, Pallas kernels: 48.9 us -> 51.4 us  [fused(): pl.pallas_call(fused_kernel, out_shape=jax.ShapeDtypeStruct((channels, le...]
where the time goes in v5:
time: 55.2 us; the launch traced here: 55 us
  Pallas kernels  51.4 us (93%)
  other arithmetic  1.97 us (4%)
  local copies, waits for them, and re-layouts  1.62 us (3%)
    pallas_call x1, Pallas kernels, fused(): pl.pallas_call(fused_kernel, out_shape=jax.ShapeDtypeStruct((channels, le...  51.4 us
    convert_element_type x1, other arithmetic, on_device(): return (second_conv.astype(jnp.float32) * gate_two).astype(jnp.bfloat16)  1.97 us

profile of v5, /device:TPU:9, one launch (start us, length us, event | category | flops | bytes accessed | tf_op | source)
XLA Modules:
  0.0 55.0 jit_solution(1543769624678943955)
XLA Ops:
  0.0 0.0 copy-start
  0.0 0.8 %dynamic_slice.3 = f32[256]{0:T(256)S(1)} dynamic-slice(f32[2048]{0:T(1024)} %param.15, s32[]{:T(128)S(6)} %select_n.3), dynamic_slice_sizes={256} | dynamic-slice | bytes 2052 | tf_op jit(solution)/shard_map/dynamic_slice | solution.py:396
  0.8 0.8 %copy.12.skip = f32[256,1]{1,0:T(8,128)} copy(f32[256,1]{0,1:T(1,128)S(1)} %bitcast.1) | data formatting | bytes 2048 | tf_op jit(solution)/shard_map/broadcast_in_dim | solution.py:396
  1.6 51.4 %shard_map.109 = bf16[2048,128]{1,0:T(8,128)(2,1)} custom-call(bf16[2048,128]{1,0:T(8,128)(2,1)} %features_hbm.1, bf16[2048,128]{1,0:T(8,128)(2,1)} %gate_hbm.1, bf16[2048,128]{1,0:T(8,128)(2,1)} %taps_hbm.1, bf16[2048,128]{1,0:T(8,128)(2,1)} %long_filter.1, bf16[2048,128]{1,0:T(8,128)(2,1)} %taps_two.1, bf16[256,256]{1,0:T(8,128)(2,1)} %constant.25.clone.short_high_hbm, ...), custom_call_target="tpu_custom_call" | custom-call | tf_op jit(solution)/shard_map/pallas_call | solution.py:351
  53.1 0.0 copy-done
  53.1 2.0 %multiply_convert_fusion = bf16[2048,128]{1,0:T(8,128)(2,1)} fusion(bf16[2048,128]{1,0:T(8,128)(2,1)S(1)} %copy-done, bf16[2048,128]{1,0:T(8,128)(2,1)} %shard_map.109), kind=kLoop, calls=%fused_computation | loop fusion | flops 1048576 | bytes 1572864 | tf_op jit(solution)/shard_map/convert_element_type | solution.py:402
Async XLA Ops:
  0.0 53.1 %copy-start = (bf16[2048,128]{1,0:T(8,128)(2,1)S(1)}, bf16[2048,128]{1,0:T(8,128)(2,1)}, u32[]{:S(2)}) copy-start(bf16[2048,128]{1,0:T(8,128)(2,1)} %param.17) | copy-start | bytes 1572868
